TPU v7x, 32 devices: a whole 2x2x4 slice. The times are simulated.
32 devices in a mesh: replica: 8 (over z, y), fsdp: 4 (over x, core).
Axes of the slice: x: 2, y: 2, z: 4, core: 2. Of those that a mesh axis runs over, the one named last changes fastest.
Arguments:
- local_weights: float32 [8, 5120, 512], P('replica', 'fsdp')
- outer_base: float32 [5120, 512], P('fsdp')
- outer_momentum: float32 [5120, 512], P(('fsdp', 'replica')), may hold values from -4 to 4
- batch: bfloat16 [8, 2, 1536, 5120], P('replica', None, 'fsdp'), may hold values from -6 to 6
- cotangent: bfloat16 [8, 2, 1536, 512], P('replica', None, 'fsdp'), may hold values from -6 to 6
- step: int32 [1], replicated, may hold values from 0 to 4095
- plan: int32 [8], replicated, may hold values from 0 to 3
Outputs:
- new_weights: float32 [8, 5120, 512], P('replica', 'fsdp')
- new_base: float32 [5120, 512], P('fsdp')
- new_momentum: float32 [5120, 512], P(('fsdp', 'replica'))
All inputs are finite; a program needn't handle non-finite values. Where the computation divides by a largest or mean magnitude, that divisor is 1e-20 or more.
Results may differ from a plain program's by a relative error of at most 0.0055.
Values may be sent and summed in bfloat16 or wider, within the bound.
A program may use at most 128 MiB of HBM per device.

v0:
```python
import jax
import jax.numpy as jnp
from jax import lax
from jax.sharding import PartitionSpec as P

D = 5120
HEAD_DIM = 128
SCHED_LEN = 8
INNER = 2


eps_norm = 1e-06
eps_scale = 1e-06
inner_rate = 0.5
outer_rate = 0.7
outer_decay = 0.9
mix_local = 0.5


def pick_fragment(step, plan):
    position = step[0] % SCHED_LEN
    hits = jnp.arange(SCHED_LEN, dtype=jnp.int32) == position
    return jnp.sum(jnp.where(hits, plan, 0))


def rate_of(step):
    return outer_rate * 1024.0 / (1024.0 + step[0].astype(jnp.float32))


def normalize(rows):
    values = rows.astype(jnp.float32)
    mean_square = jnp.mean(values * values, axis=-1, keepdims=True)
    return (values * lax.rsqrt(mean_square + eps_norm)).astype(jnp.bfloat16)


def silu_slope(values):
    gate_value = jax.nn.sigmoid(values)
    return gate_value * (1.0 + values * (1.0 - gate_value))


def on_device(local_weights, outer_base, outer_momentum, batch, cotangent, step, plan):
    inv_width = D ** (-0.5)
    fragment = pick_fragment(step, plan)
    outer_lr = rate_of(step)
    first_col = fragment * HEAD_DIM
    weights = local_weights[0]
    base_cols = lax.dynamic_slice_in_dim(outer_base, first_col, HEAD_DIM, 1)
    pseudo_grad = base_cols - lax.dynamic_slice_in_dim(weights, first_col, HEAD_DIM, 1)
    block_scale = (jnp.max(jnp.abs(pseudo_grad), axis=1) + eps_scale).astype(jnp.bfloat16)
    codes_out = (pseudo_grad / block_scale.astype(jnp.float32)[:, None]).astype(jnp.bfloat16)
    moment_cols = lax.dynamic_slice_in_dim(outer_momentum, first_col, HEAD_DIM, 1)
    share_rows = moment_cols.shape[0]
    share_first = lax.axis_index("replica") * share_rows
    replicas = lax.axis_size("replica")
    dequant = (
        lax.all_gather(codes_out[None], "replica", axis=0, tiled=True).astype(jnp.float32)
        * lax.all_gather(block_scale[None], "replica", axis=0, tiled=True).astype(jnp.float32)[
            :, :, None
        ]
    )
    running = jnp.sum(dequant, axis=0)
    average = running / replicas
    moment_all = lax.all_gather(moment_cols, "replica", axis=0, tiled=True)
    moment_full = outer_decay * moment_all + average
    base_frag = base_cols - outer_lr * (outer_decay * moment_full + average)
    moment_new = lax.dynamic_slice_in_dim(moment_full, share_first, share_rows, 0)
    for index in range(INNER):
        normed = normalize(batch[0, index])
        cot_rows = cotangent[0, index].astype(jnp.float32)
        values = (
            jnp.dot(
                normed,
                lax.all_gather(weights.astype(jnp.bfloat16), "fsdp", axis=0, tiled=True),
                preferred_element_type=jnp.float32,
            )
            * inv_width
        )
        slopes = (cot_rows * silu_slope(values)).astype(jnp.bfloat16)
        gradient = lax.psum_scatter(
            jnp.dot(normed.T, slopes, preferred_element_type=jnp.float32).astype(jnp.bfloat16),
            "fsdp",
            scatter_dimension=0,
            tiled=True,
        ).astype(jnp.float32)
        weights = weights - inner_rate * inv_width * gradient
    trained_cols = lax.dynamic_slice_in_dim(weights, first_col, HEAD_DIM, 1)
    blended = mix_local * trained_cols + (1.0 - mix_local) * base_frag
    new_weights = lax.dynamic_update_slice_in_dim(weights, blended, first_col, 1)[None]
    new_base = lax.dynamic_update_slice_in_dim(outer_base, base_frag, first_col, 1)
    new_momentum = lax.dynamic_update_slice_in_dim(outer_momentum, moment_new, first_col, 1)
    return (new_weights, new_base, new_momentum)


def solution(mesh):
    placed = (
        P("replica", "fsdp", None),
        P("fsdp", None),
        P(("fsdp", "replica"), None),
        P("replica", None, "fsdp", None),
        P("replica", None, "fsdp", None),
        P(),
        P(),
    )
    return jax.shard_map(
        on_device,
        mesh=mesh,
        in_specs=placed,
        out_specs=(P("replica", "fsdp", None), P("fsdp", None), P(("fsdp", "replica"), None)),
        check_vma=False,
    )
```

profile of v0, /device:TPU:0, one launch (start us, length us, event | category | flops | bytes accessed | tf_op | source)
XLA Modules:
  0.0 291.7 jit_solution(2048584347973005105)
XLA Ops:
  7.2 0.0 all-gather.7.cloned.1.call-start
  7.2 3.6 %copy.19 = f32[1280,512]{1,0:T(8,128)} copy(f32[1280,512]{1,0:T(8,128)} %param.8) | data formatting | bytes 5242880
  10.9 1.2 bitcast_convert_fusion
  12.2 0.0 reduce-scatter.3.cloned.1.call-start
  12.2 4.2 %fusion = (f32[384]{0:T(512)S(1)}, f32[384]{0:T(512)S(1)}) fusion(bf16[1,2,384,5120]{3,2,1,0:T(8,128)(2,1)} %param.10), kind=kLoop, calls=%fused_computation.4 | loop fusion | flops 11795712 | bytes 7867392 | tf_op jit(solution)/shard_map/reduce_sum | solution.py:32
  16.4 39.1 %all-gather.7.cloned.1.call-done = bf16[5120,512]{1,0:T(8,128)(2,1)} async-done(((bf16[1280,512]{1,0:T(8,128)(2,1)}), bf16[5120,512]{1,0:T(8,128)(2,1)}) %all-gather.7.cloned.1.call-update) | async-done | bytes 5242896 | tf_op jit(solution)/shard_map/all_gather | solution.py:73
  55.5 12.5 %convolution_convert_fusion.1 = bf16[5120,512]{1,0:T(8,128)(2,1)} fusion(f32[384]{0:T(512)S(1)} %add_rsqrt_fusion.1, bf16[1,2,384,5120]{3,2,1,0:T(8,128)(2,1)} %param.10, bf16[5120,512]{1,0:T(8,128)(2,1)} %all-gather.7.cloned.1.call-done, bf16[1,2,384,512]{3,2,1,0:T(8,128)(2,1)} %param.11), kind=kOutput, calls=%fused_computation.9 | convolution fusion | flops 4043112448 | bytes 18747392 | tf_op jit(solution)/shard_map/dot_general | solution.py:80
  67.9 0.0 reduce-scatter.3.cloned.1.call-update
  68.0 0.0 all-gather.9.cloned.1.call-start
  68.0 51.5 %reduce-scatter.3.cloned.1.call-done = bf16[1280,512]{1,0:T(8,128)(2,1)} async-done(((bf16[5120,512]{1,0:T(8,128)(2,1)}), bf16[1280,512]{1,0:T(8,128)(2,1)}) %reduce-scatter.3.cloned.1.call-update) | async-done | bytes 1310736 | tf_op jit(solution)/shard_map/reduce_scatter | solution.py:79
  119.5 2.9 fusion.5
  122.4 0.0 all-gather.9.cloned.1.call-update
  122.4 0.0 all-gather.11.cloned.1.call-start
  123.1 0.7 fusion.28
  124.5 1.3 abs_reduce_fusion
  125.8 2.0 divide_convert_fusion
  127.9 0.2 reduce-scatter.5.cloned.1.call-start
  128.1 34.9 %all-gather.9.cloned.1.call-done = bf16[5120,512]{1,0:T(8,128)(2,1)} async-done(((bf16[1280,512]{1,0:T(8,128)(2,1)}), bf16[5120,512]{1,0:T(8,128)(2,1)}) %all-gather.9.cloned.1.call-update) | async-done | bytes 5242896 | tf_op jit(solution)/shard_map/all_gather | solution.py:73
  163.0 12.4 %convolution_convert_fusion = bf16[5120,512]{1,0:T(8,128)(2,1)} fusion(f32[384]{0:T(512)S(1)} %add_rsqrt_fusion, bf16[1,2,384,5120]{3,2,1,0:T(8,128)(2,1)} %param.10, bf16[5120,512]{1,0:T(8,128)(2,1)} %all-gather.9.cloned.1.call-done, bf16[1,2,384,512]{3,2,1,0:T(8,128)(2,1)} %param.11), kind=kOutput, calls=%fused_computation.8 | convolution fusion | flops 4043112448 | bytes 18747392 | tf_op jit(solution)/shard_map/dot_general | solution.py:80
  175.5 30.9 %all-gather.2 = bf16[8,1,1280]{2,1,0:T(2,128)(2,1)S(1)} all-gather(bf16[1,1,1280]{2,1,0:T(2,128)(2,1)S(1)} %reshape.60), channel_id=3, replica_groups=mesh['replica'=8,'fsdp'=4] {'replica'}, dimensions={0}, use_global_device_ids=true | all-gather | bytes 23040 | tf_op jit(solution)/shard_map/all_gather | solution.py:57
  206.5 34.8 %all_gather.17 = f32[1280,128]{1,0:T(8,128)} all-gather(f32[160,128]{1,0:T(8,128)S(1)} %constant_dynamic-slice_fusion), channel_id=1, replica_groups=mesh['replica'=8,'fsdp'=4] {'replica'}, dimensions={0}, use_global_device_ids=true | all-gather | bytes 737280 | tf_op jit(solution)/shard_map/all_gather | solution.py:63
  241.3 3.5 %fusion.4 = f32[1280,128]{1,0:T(8,128)S(1)} fusion(bf16[8,1280,128]{2,1,0:T(8,128)(2,1)} %bitcast.61, f32[8,1280]{1,0:T(8,128)S(1)} %bitcast.62), kind=kLoop, calls=%fused_computation.11 | loop fusion | flops 3768320 | bytes 3317760 | tf_op jit(solution)/shard_map/reduce_sum | solution.py:61
  244.8 33.5 %reduce-scatter.5.cloned.1.call-done = bf16[1280,512]{1,0:T(8,128)(2,1)} async-done(((bf16[5120,512]{1,0:T(8,128)(2,1)}), bf16[1280,512]{1,0:T(8,128)(2,1)}) %reduce-scatter.5.cloned.1.call-update) | async-done | bytes 1310736 | tf_op jit(solution)/shard_map/reduce_scatter | solution.py:79
  278.3 2.3 multiply_subtract_fusion
  280.6 0.2 copy.13
  280.9 1.5 copy-done.1
  282.4 0.1 copy-done.3
  282.5 0.3 bitcast_dynamic-update-slice_fusion
  282.8 0.3 multiply_add_fusion
  283.1 0.9 dynamic-slice_dynamic-update-slice_fusion
  284.0 0.3 copy-done.4
  284.3 0.9 copy-done.2
  (23 shorter events, 0.2 us)
Async XLA Ops:
  7.2 3.7 %copy-start = (f32[1,1280,512]{2,1,0:T(8,128)S(1)}, f32[1,1280,512]{2,1,0:T(8,128)}, u32[]{:S(2)}) copy-start(f32[1,1280,512]{2,1,0:T(8,128)} %param.7) | copy-start | bytes 7864324
  7.2 3.7 %copy-start.6 = (f32[160,512]{1,0:T(8,128)S(1)}, f32[160,512]{1,0:T(8,128)}, u32[]{:S(2)}) copy-start(f32[160,512]{1,0:T(8,128)} %param.9) | copy-start | bytes 983044
  7.2 48.3 %all-gather.7.cloned.1.call-start = ((), (), s32[]{:S(2)}) async-start(), calls=%async_computation.2 | async-start | bytes 6553600 | tf_op jit(solution)/shard_map/all_gather | solution.py:73
  10.9 195.6 %copy-start.5 = (f32[160,512]{1,0:T(8,128)}, f32[160,512]{1,0:T(8,128)S(1)}, u32[]{:S(2)}) copy-start(f32[160,512]{1,0:T(8,128)S(1)} %copy.20) | copy-start | bytes 983044
  12.2 107.3 %reduce-scatter.3.cloned.1.call-start = ((), (), s32[]{:S(2)}) async-start(), calls=%async_computation.3 | async-start | bytes 6553600 | tf_op jit(solution)/shard_map/reduce_scatter | solution.py:79
  68.0 55.1 %copy-start.7 = (s32[8]{0:T(128)S(1)}, s32[8]{0:T(128)}, u32[]{:S(2)}) copy-start(s32[8]{0:T(128)} %param.13) | copy-start | bytes 100
  68.0 95.0 %all-gather.9.cloned.1.call-start = ((), (), s32[]{:S(2)}) async-start(), calls=%async_computation.4 | async-start | bytes 6553600 | tf_op jit(solution)/shard_map/all_gather | solution.py:73
  122.4 118.9 %all-gather.11.cloned.1.call-start = ((), (), s32[]{:S(2)}) async-start(), calls=%async_computation.6 | async-start | bytes 2949120 | tf_op jit(solution)/shard_map/all_gather | solution.py:56
  127.9 150.4 %reduce-scatter.5.cloned.1.call-start = ((), (), s32[]{:S(2)}) async-start(), calls=%async_computation.5 | async-start | bytes 6553600 | tf_op jit(solution)/shard_map/reduce_scatter | solution.py:79
  280.6 1.7 copy-start.1
  280.6 1.9 copy-start.3
  282.8 1.5 copy-start.4
  283.0 2.1 copy-start.2
Sparse Core Ops, SparseCore 0:
  12.3 43.1 all-gather.6
  68.1 51.3 reduce-scatter.2
  122.5 40.4 all-gather.8
  165.3 60.5 all-gather.10
  228.4 49.8 reduce-scatter.4
where the time goes:
time: 292 us
  waiting for transfers between devices  159 us (54%)
  blocking collectives  65.7 us (22%)
  matrix products  24.9 us (9%)
  other arithmetic  18.6 us (6%)
  between operations  15.3 us (5%)
  local copies, waits for them, and re-layouts  7.66 us (3%)
    reduce_scatter x2, waiting for transfers between devices, on_device(): lax.psum_scatter(jnp.dot(normed.T, slopes, preferred_element_type=jnp.flo...  85 us
    all_gather x2, waiting for transfers between devices, on_device(): lax.all_gather(weights.astype(jnp.bfloat16), 'fsdp', axis=0, tiled=True)  73.9 us
    all_gather x1, blocking collectives, on_device(): moment_all = lax.all_gather(moment_cols, 'replica', axis=0, tiled=True)  34.8 us
    all_gather x1, blocking collectives, on_device(): lax.all_gather(block_scale[None], 'replica', axis=0, tiled=True)  30.9 us
    dot_general x2, matrix products, on_device(): jnp.dot(normed.T, slopes, preferred_element_type=jnp.float32)  24.9 us
    unnamed x21, local copies, waits for them, and re-layouts  6.75 us
  transfers between devices with their start and end apart: 5, of which 4 were waited for; matrix products, arithmetic and copies ran while one was open for 8% of the time, Pallas kernels for 0%

commit v1 on v0

--- a/solution.py
+++ b/solution.py
@@ -1,12 +1,15 @@
 import jax
 import jax.numpy as jnp
 from jax import lax
+from jax.experimental import pallas as pl
+from jax.experimental.pallas import tpu as pltpu
 from jax.sharding import PartitionSpec as P
 
 D = 5120
 HEAD_DIM = 128
 SCHED_LEN = 8
 INNER = 2
+MESH = pl.DeviceIdType.MESH
 
 
 eps_norm = 1e-06
@@ -91,6 +94,362 @@
     return (new_weights, new_base, new_momentum)
 
 
+def fused_kernel(
+    step_ref, plan_ref, weights_hbm, base_hbm, moment_hbm, batch_hbm, cot_hbm,
+    new_weights_hbm, new_base_hbm, new_moment_hbm,
+    weights, base, moment, normed, turned, full, cot, slopes,
+    part_out, part_in, part_far, part_own, sum_out, sum_in,
+    shares, shares_in, frag_rows,
+    load_sem, store_sem, gather_send, gather_recv, part_send, part_recv,
+    share_send, share_recv, frag_send, frag_recv,
+):
+    inner, shards, tokens, depth = normed.shape
+    halves, width = full.shape[2], full.shape[4]
+    replicas, share_rows = shares.shape[0], shares.shape[1]
+    inv_width = (shards * depth) ** (-0.5)
+    rate = inner_rate * inv_width
+    me = lax.axis_index("fsdp")
+    my_replica = lax.axis_index("replica")
+    chip, core = me // 2, me % 2
+    partner = chip * 2 + (1 - core)
+    across = (1 - chip) * 2 + core
+    diagonal = (1 - chip) * 2 + (1 - core)
+
+    def peer(offset):
+        return lax.rem(my_replica + offset, replicas)
+
+    def block_cols(half):
+        return pl.ds(half * width, width)
+
+    loads = []
+
+    def load(src, dst):
+        copy = pltpu.make_async_copy(src, dst, load_sem.at[len(loads)])
+        copy.start()
+        loads.append(copy)
+        return copy
+
+    load_w = [load(weights_hbm.at[:, block_cols(h)], weights.at[:, block_cols(h)]) for h in range(halves)]
+    load_x = [
+        [load(batch_hbm.at[k, :, pl.ds(o * depth, depth)], normed.at[k, o]) for o in range(shards)]
+        for k in range(inner)
+    ]
+    load_base = load(base_hbm, base)
+    load_moment = load(moment_hbm, moment)
+    load_cot = load(cot_hbm, cot)
+
+    barrier = pltpu.get_barrier_semaphore()
+    for other in (partner, across):
+        pl.semaphore_signal(barrier, inc=1, device_id={"fsdp": other}, device_id_type=MESH)
+    for offset in range(1, replicas):
+        pl.semaphore_signal(barrier, inc=1, device_id={"replica": peer(offset)}, device_id_type=MESH)
+    pl.semaphore_wait(barrier, replicas + 1)
+
+    started = []
+
+    def send(src, dst, send_sem, recv_sem, target):
+        copy = pltpu.make_async_remote_copy(
+            src_ref=src, dst_ref=dst, send_sem=send_sem, recv_sem=recv_sem,
+            device_id=target, device_id_type=MESH,
+        )
+        copy.start()
+        started.append(copy)
+        return copy
+
+    def slot(k, h, i):
+        return (k * halves + h) * 3 + i
+
+    gathers, partials, sums = {}, {}, {}
+
+    def gather_start(k, h):
+        full[k, me, h] = weights[:, h * width : (h + 1) * width].astype(jnp.bfloat16)
+        mine = full.at[k, me, h]
+        gathers[k, h] = [
+            send(mine, mine, gather_send.at[slot(k, h, i)], gather_recv.at[slot(k, h, i)], {"fsdp": target})
+            for i, target in enumerate((across, partner))
+        ]
+
+    def gather_finish(k, h):
+        gathers[k, h][0].wait_recv()
+        theirs = full.at[k, across, h]
+        forward = send(
+            theirs, theirs, gather_send.at[slot(k, h, 2)], gather_recv.at[slot(k, h, 2)], {"fsdp": partner}
+        )
+        gathers[k, h][1].wait_recv()
+        forward.wait_recv()
+
+    def normalize_rows(k):
+        rows = 16
+
+        @pl.loop(0, tokens // rows)
+        def _(i):
+            at = pl.ds(pl.multiple_of(i * rows, rows), rows)
+            total = jnp.zeros((rows, 1), jnp.float32)
+            for o in range(shards):
+                x = normed[k, o, at, :].astype(jnp.float32)
+                total = total + jnp.sum(x * x, axis=-1, keepdims=True)
+            scale = lax.rsqrt(total * (1.0 / (shards * depth)) + eps_norm)
+            for o in range(shards):
+                x = normed[k, o, at, :].astype(jnp.float32)
+                normed[k, o, at, :] = (x * scale).astype(jnp.bfloat16)
+
+    tile = 256
+
+    def turn(k):
+        for o in range(shards):
+
+            @pl.loop(0, depth // tile)
+            def _(b):
+                at = pl.ds(pl.multiple_of(b * tile, tile), tile)
+                turned[o, at, :] = normed[k, o, :, at].T
+
+    def forward(k, h):
+        def add(o, total):
+            return total + jnp.dot(normed[k, o], full[k, o, h], preferred_element_type=jnp.float32)
+
+        values = lax.fori_loop(0, shards, add, jnp.zeros((tokens, width), jnp.float32)) * inv_width
+        cot_rows = cot[k, :, h * width : (h + 1) * width].astype(jnp.float32)
+        slopes[...] = (cot_rows * silu_slope(values)).astype(jnp.bfloat16)
+
+    def product(owner, dst):
+        @pl.loop(0, depth // tile)
+        def _(b):
+            at = pl.ds(pl.multiple_of(b * tile, tile), tile)
+            dst[at, :] = jnp.dot(
+                turned[owner, at, :], slopes[...], preferred_element_type=jnp.float32
+            ).astype(jnp.bfloat16)
+
+    def gradient_start(k, h):
+        sent = []
+        for i, owner in enumerate((diagonal, partner)):
+            product(owner, part_out.at[k, h, i])
+            sent.append(
+                send(
+                    part_out.at[k, h, i], part_in.at[k, h, i],
+                    part_send.at[slot(k, h, i)], part_recv.at[slot(k, h, i)], {"fsdp": partner},
+                )
+            )
+        partials[k, h] = sent
+        product(across, part_far)
+        sent[0].wait_recv()
+        sum_out[k, h] = (part_far[...].astype(jnp.float32) + part_in[k, h, 0].astype(jnp.float32)).astype(
+            jnp.bfloat16
+        )
+        sums[k, h] = send(
+            sum_out.at[k, h], sum_in.at[k, h],
+            part_send.at[slot(k, h, 2)], part_recv.at[slot(k, h, 2)], {"fsdp": across},
+        )
+        product(me, part_own.at[h])
+
+    def gradient_finish(k, h):
+        partials[k, h][1].wait_recv()
+        sums[k, h].wait_recv()
+        gradient = (
+            part_own[h].astype(jnp.float32)
+            + part_in[k, h, 1].astype(jnp.float32)
+            + sum_in[k, h].astype(jnp.float32)
+        )
+        cols = slice(h * width, (h + 1) * width)
+        weights[:, cols] = weights[:, cols] - rate * gradient
+
+    fragment = plan_ref[lax.rem(step_ref[0], SCHED_LEN)]
+    fragments = base.shape[1] // HEAD_DIM
+
+    def chosen(rows, index):
+        return jnp.full((rows, HEAD_DIM), fragment, jnp.int32) == index
+
+    def pick(ref, at, rows):
+        found = ref[at, 0:HEAD_DIM]
+        for j in range(1, fragments):
+            found = jnp.where(chosen(rows, j), ref[at, j * HEAD_DIM : (j + 1) * HEAD_DIM], found)
+        return found
+
+    def share_at(r):
+        return pl.ds(pl.multiple_of(r * share_rows, share_rows), share_rows)
+
+    def share_start():
+        @pl.loop(0, replicas)
+        def _(r):
+            at = share_at(r)
+            pseudo_grad = pick(base, at, share_rows) - pick(weights, at, share_rows)
+            top = jnp.max(jnp.abs(pseudo_grad), axis=1, keepdims=True) + eps_scale
+            scale = jnp.broadcast_to(top, pseudo_grad.shape).astype(jnp.bfloat16).astype(jnp.float32)
+            codes = (pseudo_grad / scale).astype(jnp.bfloat16).astype(jnp.float32)
+            shares[r] = codes * scale
+
+        return [
+            send(
+                shares.at[peer(t)], shares_in.at[t - 1],
+                share_send.at[t - 1], share_recv.at[t - 1], {"replica": peer(t)},
+            )
+            for t in range(1, replicas)
+        ]
+
+    def fragment_start(sent):
+        running = shares[my_replica]
+        for t in range(1, replicas):
+            sent[t - 1].wait_recv()
+            running = running + shares_in[t - 1]
+        average = running / replicas
+        outer_lr = (outer_rate * 1024.0) / (
+            1024.0 + jnp.full((share_rows, HEAD_DIM), step_ref[0], jnp.int32).astype(jnp.float32)
+        )
+        everything = slice(0, share_rows)
+        moment_new = outer_decay * pick(moment, everything, share_rows) + average
+        frag_rows[my_replica] = pick(base, share_at(my_replica), share_rows) - outer_lr * (
+            outer_decay * moment_new + average
+        )
+        for j in range(fragments):
+            cols = slice(j * HEAD_DIM, (j + 1) * HEAD_DIM)
+            moment[:, cols] = jnp.where(chosen(share_rows, j), moment_new, moment[:, cols])
+        return [
+            send(
+                frag_rows.at[my_replica], frag_rows.at[my_replica],
+                frag_send.at[t - 1], frag_recv.at[t - 1], {"replica": peer(t)},
+            )
+            for t in range(1, replicas)
+        ]
+
+    def fragment_finish(sent):
+        for copy in sent:
+            copy.wait_recv()
+
+        @pl.loop(0, replicas)
+        def _(r):
+            at = share_at(r)
+            for j in range(fragments):
+                cols = slice(j * HEAD_DIM, (j + 1) * HEAD_DIM)
+                base[at, cols] = jnp.where(chosen(share_rows, j), frag_rows[r], base[at, cols])
+
+    def blend(h):
+        @pl.loop(0, replicas)
+        def _(r):
+            at = share_at(r)
+            for j in range(h * width // HEAD_DIM, (h + 1) * width // HEAD_DIM):
+                cols = slice(j * HEAD_DIM, (j + 1) * HEAD_DIM)
+                trained = weights[at, cols]
+                mixed = mix_local * trained + (1.0 - mix_local) * frag_rows[r]
+                weights[at, cols] = jnp.where(chosen(share_rows, j), mixed, trained)
+
+    for h in range(halves):
+        load_w[h].wait()
+        gather_start(0, h)
+    load_base.wait()
+    share_sent = share_start()
+    frag_sent = None
+    stores = []
+    for k in range(inner):
+        if k == 0:
+            for copy in load_x[0]:
+                copy.wait()
+            normalize_rows(0)
+            turn(0)
+            load_cot.wait()
+        for h in range(halves):
+            gather_finish(k, h)
+            forward(k, h)
+            gradient_start(k, h)
+            if k == 0 and h == 0:
+                for copy in load_x[1]:
+                    copy.wait()
+                normalize_rows(1)
+        if k + 1 < inner:
+            turn(k + 1)
+        if k == 0:
+            load_moment.wait()
+            frag_sent = fragment_start(share_sent)
+        for h in range(halves):
+            gradient_finish(k, h)
+            if k + 1 < inner:
+                gather_start(k + 1, h)
+            else:
+                blend(h)
+                copy = pltpu.make_async_copy(
+                    weights.at[:, block_cols(h)], new_weights_hbm.at[:, block_cols(h)], store_sem.at[h]
+                )
+                copy.start()
+                stores.append(copy)
+        if k == 0:
+            fragment_finish(frag_sent)
+            for i, (src, dst) in enumerate(((base, new_base_hbm), (moment, new_moment_hbm))):
+                copy = pltpu.make_async_copy(src, dst, store_sem.at[halves + i])
+                copy.start()
+                stores.append(copy)
+    for copy in started:
+        copy.wait_send()
+    for copy in stores:
+        copy.wait()
+
+
+def fused(local_weights, outer_base, outer_momentum, batch, cotangent, step, plan):
+    rows, columns = outer_base.shape
+    inner, tokens, features = batch.shape[1:]
+    shards, replicas = features // rows, rows // outer_momentum.shape[0]
+    share_rows = outer_momentum.shape[0]
+    halves = 2
+    width = columns // halves
+    f32, bf16 = jnp.float32, jnp.bfloat16
+    hbm = pl.BlockSpec(memory_space=pl.ANY)
+    smem = pl.BlockSpec(memory_space=pltpu.SMEM)
+    dma = pltpu.SemaphoreType.DMA
+    flops = inner * 4 * tokens * features * columns
+    return pl.pallas_call(
+        fused_kernel,
+        out_shape=(
+            jax.ShapeDtypeStruct((rows, columns), f32),
+            jax.ShapeDtypeStruct((rows, columns), f32),
+            jax.ShapeDtypeStruct((share_rows, columns), f32),
+        ),
+        in_specs=[smem, smem] + [hbm] * 5,
+        out_specs=(hbm,) * 3,
+        scratch_shapes=[
+            pltpu.VMEM((rows, columns), f32),
+            pltpu.VMEM((rows, columns), f32),
+            pltpu.VMEM((share_rows, columns), f32),
+            pltpu.VMEM((inner, shards, tokens, rows), bf16),
+            pltpu.VMEM((shards, rows, tokens), bf16),
+            pltpu.VMEM((inner, shards, halves, rows, width), bf16),
+            pltpu.VMEM((inner, tokens, columns), bf16),
+            pltpu.VMEM((tokens, width), bf16),
+            pltpu.VMEM((inner, halves, 2, rows, width), bf16),
+            pltpu.VMEM((inner, halves, 2, rows, width), bf16),
+            pltpu.VMEM((rows, width), bf16),
+            pltpu.VMEM((halves, rows, width), bf16),
+            pltpu.VMEM((inner, halves, rows, width), bf16),
+            pltpu.VMEM((inner, halves, rows, width), bf16),
+            pltpu.VMEM((replicas, share_rows, HEAD_DIM), f32),
+            pltpu.VMEM((replicas - 1, share_rows, HEAD_DIM), f32),
+            pltpu.VMEM((replicas, share_rows, HEAD_DIM), f32),
+            dma((halves + inner * shards + 3,)),
+            dma((halves + 2,)),
+            dma((inner * halves * 3,)),
+            dma((inner * halves * 3,)),
+            dma((inner * halves * 3,)),
+            dma((inner * halves * 3,)),
+            dma((replicas - 1,)),
+            dma((replicas - 1,)),
+            dma((replicas - 1,)),
+            dma((replicas - 1,)),
+        ],
+        compiler_params=pltpu.CompilerParams(
+            collective_id=0, has_side_effects=True, vmem_limit_bytes=60 * 2**20
+        ),
+        cost_estimate=pl.CostEstimate(
+            flops=flops, bytes_accessed=20 * 2**20, transcendentals=inner * tokens * columns
+        ),
+    )(step, plan, local_weights[0], outer_base, outer_momentum, batch[0], cotangent[0])
+
+
+def on_device_fused(*args):
+    new_weights, new_base, new_momentum = fused(*args)
+    return (new_weights[None], new_base, new_momentum)
+
+
+def fits(mesh):
+    shards, replicas = mesh.shape["fsdp"], mesh.shape["replica"]
+    return shards == 4 and (D // (shards * replicas)) % 8 == 0
+
+
 def solution(mesh):
     placed = (
         P("replica", "fsdp", None),
@@ -102,7 +461,7 @@
         P(),
     )
     return jax.shard_map(
-        on_device,
+        on_device_fused if fits(mesh) else on_device,
         mesh=mesh,
         in_specs=placed,
         out_specs=(P("replica", "fsdp", None), P("fsdp", None), P(("fsdp", "replica"), None)),

time: 292 us -> 131 us (0.45)
  waiting for transfers between devices: 159 us -> 0 us
  Pallas kernels: 0 us -> 124 us
  blocking collectives: 65.7 us -> 0 us
  matrix products: 24.9 us -> 0 us
  other arithmetic: 18.6 us -> 0 us
  between operations: 15.3 us -> 1.3 us
    pallas_call x0 -> x1, Pallas kernels: none -> 124 us  [fused(): pl.pallas_call(fused_kernel, out_shape=(jax.ShapeDtypeStruct((rows, colum...]
    reduce_scatter x2 -> x0, waiting for transfers between devices: 85 us -> none  [on_device(): lax.psum_scatter(jnp.dot(normed.T, slopes, preferred_element_type=jnp.flo...]
    all_gather x3 -> x0, waiting for transfers between devices: 73.9 us -> none  [the longest x2 73.9 us: on_device(): lax.all_gather(weights.astype(jnp.bfloat16), 'fsdp', axis=0, tiled=True)]
    all_gather x2 -> x0, blocking collectives: 65.7 us -> none  [the longest x1 34.8 us: on_device(): moment_all = lax.all_gather(moment_cols, 'replica', axis=0, tiled=True)]
    dot_general x2 -> x0, matrix products: 24.9 us -> none  [on_device(): jnp.dot(normed.T, slopes, preferred_element_type=jnp.float32)]
    reduce_sum x3 -> x0, other arithmetic: 8.31 us -> none  [the longest x1 4.16 us: normalize(): mean_square = jnp.mean(values * values, axis=-1, keepdims=True)]
    convert_element_type x4 -> x0, other arithmetic: 6.14 us -> none  [the longest x2 4.09 us: on_device(): weights.astype(jnp.bfloat16)]
    unnamed x21 -> x7, local copies, waits for them, and re-layouts: 6.75 us -> 5.84 us
  transfers between devices with their start and end apart: 5 -> 0, of which waited for: 4 -> 0; matrix products, arithmetic and copies ran while one was open for 8% -> 0% of each run, Pallas kernels for 0% -> 0%
where the time goes in v1:
time: 131 us
  Pallas kernels  124 us (95%)
  local copies, waits for them, and re-layouts  5.84 us (4%)
    pallas_call x1, Pallas kernels, fused(): pl.pallas_call(fused_kernel, out_shape=(jax.ShapeDtypeStruct((rows, colum...  124 us
    unnamed x7, local copies, waits for them, and re-layouts  5.84 us

profile of v1, /device:TPU:0, one launch (start us, length us, event | category | flops | bytes accessed | tf_op | source)
XLA Modules:
  0.0 130.7 jit_solution(15329575536418220764)
XLA Ops:
  1.3 123.6 %shard_map.94 = (f32[1280,512]{1,0:T(8,128)}, f32[1280,512]{1,0:T(8,128)}, f32[160,512]{1,0:T(8,128)}) custom-call(s32[1]{0:T(128)S(6)} %copy.13.step_ref, s32[8]{0:T(128)} %plan_ref.1, f32[1280,512]{1,0:T(8,128)} %bitcast.6, f32[1280,512]{1,0:T(8,128)} %base_hbm.1, f32[160,512]{1,0:T(8,128)} %moment_hbm.1, bf16[2,384,5120]{2,1,0:T(8,128)(2,1)} %bitcast.5, ...), custom_call_target="tpu_custom_call" | custom-call | flops 8053063680 | bytes 20971520 | tf_op jit(solution)/shard_map/pallas_call | solution.py:396
  124.9 0.0 copy-start
  124.9 3.6 %copy.14 = f32[1,1280,512]{2,1,0:T(8,128)} copy(f32[1,1280,512]{2,1,0:T(8,128)} %bitcast.4) | data formatting | bytes 5242880
  128.5 0.0 copy-done
  128.5 0.0 copy-start.1
  128.5 1.5 %copy.15 = f32[1280,512]{1,0:T(8,128)} copy(f32[1280,512]{1,0:T(8,128)S(1)} %copy-done) | data formatting | bytes 5242880
  130.0 0.0 copy-done.1
  130.0 0.7 copy.16
Async XLA Ops:
  124.9 3.6 %copy-start = (f32[1280,512]{1,0:T(8,128)S(1)}, f32[1280,512]{1,0:T(8,128)}, u32[]{:S(2)}) copy-start(f32[1280,512]{1,0:T(8,128)} %get-tuple-element.13) | copy-start | bytes 7864324
  128.5 1.5 %copy-start.1 = (f32[160,512]{1,0:T(8,128)S(1)}, f32[160,512]{1,0:T(8,128)}, u32[]{:S(2)}) copy-start(f32[160,512]{1,0:T(8,128)} %get-tuple-element.14) | copy-start | bytes 983044

commit v2 on v1

--- a/solution.py
+++ b/solution.py
@@ -96,11 +96,11 @@
 
 def fused_kernel(
     step_ref, plan_ref, weights_hbm, base_hbm, moment_hbm, batch_hbm, cot_hbm,
-    new_weights_hbm, new_base_hbm, new_moment_hbm,
-    weights, base, moment, normed, turned, full, cot, slopes,
+    weights, base, moment,
+    normed, turned, full, cot, total, slopes,
     part_out, part_in, part_far, part_own, sum_out, sum_in,
     shares, shares_in, frag_rows,
-    load_sem, store_sem, gather_send, gather_recv, part_send, part_recv,
+    load_sem, gather_send, gather_recv, part_send, part_recv,
     share_send, share_recv, frag_send, frag_recv,
 ):
     inner, shards, tokens, depth = normed.shape
@@ -129,7 +129,16 @@
         loads.append(copy)
         return copy
 
-    load_w = [load(weights_hbm.at[:, block_cols(h)], weights.at[:, block_cols(h)]) for h in range(halves)]
+    def load_half(h):
+        return load(weights_hbm.at[:, block_cols(h)], weights.at[:, block_cols(h)])
+
+    load_w = [load_half(0)]
+    barrier = pltpu.get_barrier_semaphore()
+    for other in (partner, across):
+        pl.semaphore_signal(barrier, inc=1, device_id={"fsdp": other}, device_id_type=MESH)
+    for offset in range(1, replicas):
+        pl.semaphore_signal(barrier, inc=1, device_id={"replica": peer(offset)}, device_id_type=MESH)
+    load_w += [load_half(h) for h in range(1, halves)]
     load_x = [
         [load(batch_hbm.at[k, :, pl.ds(o * depth, depth)], normed.at[k, o]) for o in range(shards)]
         for k in range(inner)
@@ -138,13 +147,6 @@
     load_moment = load(moment_hbm, moment)
     load_cot = load(cot_hbm, cot)
 
-    barrier = pltpu.get_barrier_semaphore()
-    for other in (partner, across):
-        pl.semaphore_signal(barrier, inc=1, device_id={"fsdp": other}, device_id_type=MESH)
-    for offset in range(1, replicas):
-        pl.semaphore_signal(barrier, inc=1, device_id={"replica": peer(offset)}, device_id_type=MESH)
-    pl.semaphore_wait(barrier, replicas + 1)
-
     started = []
 
     def send(src, dst, send_sem, recv_sem, target):
@@ -160,23 +162,27 @@
         return (k * halves + h) * 3 + i
 
     gathers, partials, sums = {}, {}, {}
-
-    def gather_start(k, h):
+    first_rows = depth * 3 // 4 // 16 * 16
+    pieces = (pl.ds(0, first_rows), pl.ds(first_rows, depth - first_rows))
+    last_slot = inner * halves * 3
+
+    def cast_block(k, h):
         full[k, me, h] = weights[:, h * width : (h + 1) * width].astype(jnp.bfloat16)
+
+    def gather_across(k, h, split=False):
         mine = full.at[k, me, h]
-        gathers[k, h] = [
-            send(mine, mine, gather_send.at[slot(k, h, i)], gather_recv.at[slot(k, h, i)], {"fsdp": target})
-            for i, target in enumerate((across, partner))
+        if split:
+            parts = [(mine.at[rows, :], at) for rows, at in zip(pieces, (slot(k, h, 0), last_slot))]
+        else:
+            parts = [(mine, slot(k, h, 0))]
+        gathers[k, h, 0] = [
+            send(part, part, gather_send.at[at], gather_recv.at[at], {"fsdp": across}) for part, at in parts
         ]
 
-    def gather_finish(k, h):
-        gathers[k, h][0].wait_recv()
-        theirs = full.at[k, across, h]
-        forward = send(
-            theirs, theirs, gather_send.at[slot(k, h, 2)], gather_recv.at[slot(k, h, 2)], {"fsdp": partner}
-        )
-        gathers[k, h][1].wait_recv()
-        forward.wait_recv()
+    def gather_beside(k, h):
+        mine = full.at[k, me, h]
+        at = slot(k, h, 1)
+        gathers[k, h, 1] = send(mine, mine, gather_send.at[at], gather_recv.at[at], {"fsdp": partner})
 
     def normalize_rows(k):
         rows = 16
@@ -184,11 +190,11 @@
         @pl.loop(0, tokens // rows)
         def _(i):
             at = pl.ds(pl.multiple_of(i * rows, rows), rows)
-            total = jnp.zeros((rows, 1), jnp.float32)
+            squares = jnp.zeros((rows, 1), jnp.float32)
             for o in range(shards):
                 x = normed[k, o, at, :].astype(jnp.float32)
-                total = total + jnp.sum(x * x, axis=-1, keepdims=True)
-            scale = lax.rsqrt(total * (1.0 / (shards * depth)) + eps_norm)
+                squares = squares + jnp.sum(x * x, axis=-1, keepdims=True)
+            scale = lax.rsqrt(squares * (1.0 / (shards * depth)) + eps_norm)
             for o in range(shards):
                 x = normed[k, o, at, :].astype(jnp.float32)
                 normed[k, o, at, :] = (x * scale).astype(jnp.bfloat16)
@@ -204,10 +210,20 @@
                 turned[o, at, :] = normed[k, o, :, at].T
 
     def forward(k, h):
-        def add(o, total):
-            return total + jnp.dot(normed[k, o], full[k, o, h], preferred_element_type=jnp.float32)
-
-        values = lax.fori_loop(0, shards, add, jnp.zeros((tokens, width), jnp.float32)) * inv_width
+        def term(owner):
+            return jnp.dot(normed[k, owner], full[k, owner, h], preferred_element_type=jnp.float32)
+
+        for copy in gathers[k, h, 0]:
+            copy.wait_recv()
+        theirs = full.at[k, across, h]
+        at = slot(k, h, 2)
+        passed = send(theirs, theirs, gather_send.at[at], gather_recv.at[at], {"fsdp": partner})
+        total[...] = term(me)
+        gathers[k, h, 1].wait_recv()
+        total[...] += term(partner)
+        total[...] += term(across)
+        passed.wait_recv()
+        values = (total[...] + term(diagonal)) * inv_width
         cot_rows = cot[k, :, h * width : (h + 1) * width].astype(jnp.float32)
         slopes[...] = (cot_rows * silu_slope(values)).astype(jnp.bfloat16)
 
@@ -243,14 +259,14 @@
 
     def gradient_finish(k, h):
         partials[k, h][1].wait_recv()
+        cols = slice(h * width, (h + 1) * width)
+        near = part_own[h].astype(jnp.float32) + part_in[k, h, 1].astype(jnp.float32)
+        weights[:, cols] = weights[:, cols] - rate * near
         sums[k, h].wait_recv()
-        gradient = (
-            part_own[h].astype(jnp.float32)
-            + part_in[k, h, 1].astype(jnp.float32)
-            + sum_in[k, h].astype(jnp.float32)
-        )
-        cols = slice(h * width, (h + 1) * width)
-        weights[:, cols] = weights[:, cols] - rate * gradient
+        if k + 1 < inner:
+            weights[:, cols] = weights[:, cols] - rate * sum_in[k, h].astype(jnp.float32)
+        else:
+            blend(h)
 
     fragment = plan_ref[lax.rem(step_ref[0], SCHED_LEN)]
     fragments = base.shape[1] // HEAD_DIM
@@ -327,58 +343,74 @@
             at = share_at(r)
             for j in range(h * width // HEAD_DIM, (h + 1) * width // HEAD_DIM):
                 cols = slice(j * HEAD_DIM, (j + 1) * HEAD_DIM)
-                trained = weights[at, cols]
+                far = sum_in[inner - 1, h, at, j * HEAD_DIM - h * width : (j + 1) * HEAD_DIM - h * width]
+                trained = weights[at, cols] - rate * far.astype(jnp.float32)
                 mixed = mix_local * trained + (1.0 - mix_local) * frag_rows[r]
                 weights[at, cols] = jnp.where(chosen(share_rows, j), mixed, trained)
 
-    for h in range(halves):
+    load_w[0].wait()
+    cast_block(0, 0)
+    pl.semaphore_wait(barrier, replicas + 1)
+    gather_across(0, 0, split=True)
+    gather_beside(0, 0)
+    for h in range(1, halves):
         load_w[h].wait()
-        gather_start(0, h)
+        cast_block(0, h)
+        gather_beside(0, h)
+    for copy in load_x[0]:
+        copy.wait()
+    normalize_rows(0)
+    ahead = gathers[0, 0, 0][0]
+    ahead.wait_send()
+    started.remove(ahead)
+    for h in range(1, halves):
+        gather_across(0, h)
     load_base.wait()
     share_sent = share_start()
-    frag_sent = None
-    stores = []
+    turn(0)
+    load_cot.wait()
     for k in range(inner):
-        if k == 0:
-            for copy in load_x[0]:
-                copy.wait()
-            normalize_rows(0)
-            turn(0)
-            load_cot.wait()
         for h in range(halves):
-            gather_finish(k, h)
             forward(k, h)
             gradient_start(k, h)
             if k == 0 and h == 0:
                 for copy in load_x[1]:
                     copy.wait()
                 normalize_rows(1)
-        if k + 1 < inner:
+        if k == 0:
             turn(k + 1)
-        if k == 0:
             load_moment.wait()
             frag_sent = fragment_start(share_sent)
         for h in range(halves):
             gradient_finish(k, h)
             if k + 1 < inner:
-                gather_start(k + 1, h)
-            else:
-                blend(h)
-                copy = pltpu.make_async_copy(
-                    weights.at[:, block_cols(h)], new_weights_hbm.at[:, block_cols(h)], store_sem.at[h]
-                )
-                copy.start()
-                stores.append(copy)
+                cast_block(k + 1, h)
+                gather_across(k + 1, h)
+                gather_beside(k + 1, h)
         if k == 0:
             fragment_finish(frag_sent)
-            for i, (src, dst) in enumerate(((base, new_base_hbm), (moment, new_moment_hbm))):
-                copy = pltpu.make_async_copy(src, dst, store_sem.at[halves + i])
-                copy.start()
-                stores.append(copy)
     for copy in started:
         copy.wait_send()
-    for copy in stores:
+
+
+def store_kernel(weights, base, moment, new_weights, new_base, new_moment, store_sem):
+    pairs = ((weights, new_weights), (base, new_base), (moment, new_moment))
+    copies = [pltpu.make_async_copy(src, dst, store_sem.at[i]) for i, (src, dst) in enumerate(pairs)]
+    for copy in copies:
+        copy.start()
+    for copy in copies:
         copy.wait()
+
+
+def store(*results):
+    hbm = pl.BlockSpec(memory_space=pltpu.HBM)
+    return pl.pallas_call(
+        store_kernel,
+        out_shape=tuple(jax.ShapeDtypeStruct(x.shape, x.dtype) for x in results),
+        in_specs=[pl.BlockSpec(memory_space=pl.ANY)] * 3,
+        out_specs=(hbm,) * 3,
+        scratch_shapes=[pltpu.SemaphoreType.DMA((3,))],
+    )(*results)
 
 
 def fused(local_weights, outer_base, outer_momentum, batch, cotangent, step, plan):
@@ -389,27 +421,25 @@
     halves = 2
     width = columns // halves
     f32, bf16 = jnp.float32, jnp.bfloat16
-    hbm = pl.BlockSpec(memory_space=pl.ANY)
+    hbm = pl.BlockSpec(memory_space=pltpu.HBM)
     smem = pl.BlockSpec(memory_space=pltpu.SMEM)
     dma = pltpu.SemaphoreType.DMA
     flops = inner * 4 * tokens * features * columns
     return pl.pallas_call(
         fused_kernel,
         out_shape=(
-            jax.ShapeDtypeStruct((rows, columns), f32),
-            jax.ShapeDtypeStruct((rows, columns), f32),
-            jax.ShapeDtypeStruct((share_rows, columns), f32),
-        ),
-        in_specs=[smem, smem] + [hbm] * 5,
-        out_specs=(hbm,) * 3,
-        scratch_shapes=[
             pltpu.VMEM((rows, columns), f32),
             pltpu.VMEM((rows, columns), f32),
             pltpu.VMEM((share_rows, columns), f32),
+        ),
+        in_specs=[smem, smem] + [hbm] * 5,
+        out_specs=(pl.BlockSpec(memory_space=pltpu.VMEM),) * 3,
+        scratch_shapes=[
             pltpu.VMEM((inner, shards, tokens, rows), bf16),
             pltpu.VMEM((shards, rows, tokens), bf16),
             pltpu.VMEM((inner, shards, halves, rows, width), bf16),
             pltpu.VMEM((inner, tokens, columns), bf16),
+            pltpu.VMEM((tokens, width), f32),
             pltpu.VMEM((tokens, width), bf16),
             pltpu.VMEM((inner, halves, 2, rows, width), bf16),
             pltpu.VMEM((inner, halves, 2, rows, width), bf16),
@@ -421,9 +451,8 @@
             pltpu.VMEM((replicas - 1, share_rows, HEAD_DIM), f32),
             pltpu.VMEM((replicas, share_rows, HEAD_DIM), f32),
             dma((halves + inner * shards + 3,)),
-            dma((halves + 2,)),
-            dma((inner * halves * 3,)),
-            dma((inner * halves * 3,)),
+            dma((inner * halves * 3 + 1,)),
+            dma((inner * halves * 3 + 1,)),
             dma((inner * halves * 3,)),
             dma((inner * halves * 3,)),
             dma((replicas - 1,)),
@@ -432,7 +461,7 @@
             dma((replicas - 1,)),
         ],
         compiler_params=pltpu.CompilerParams(
-            collective_id=0, has_side_effects=True, vmem_limit_bytes=60 * 2**20
+            collective_id=0, has_side_effects=True, vmem_limit_bytes=52 * 2**20
         ),
         cost_estimate=pl.CostEstimate(
             flops=flops, bytes_accessed=20 * 2**20, transcendentals=inner * tokens * columns
@@ -441,7 +470,7 @@
 
 
 def on_device_fused(*args):
-    new_weights, new_base, new_momentum = fused(*args)
+    new_weights, new_base, new_momentum = store(*fused(*args))
     return (new_weights[None], new_base, new_momentum)
 
 

time: 131 us -> 297 us (2.27)
  Pallas kernels: 124 us -> 292 us
    pallas_call x1 -> x2, Pallas kernels: 124 us -> 292 us  [the longest x1 170 us: store(): pl.pallas_call(store_kernel, out_shape=tuple((jax.ShapeDtypeStruct(x.shap...]
where the time goes in v2:
time: 297 us
  Pallas kernels  292 us (98%)
  local copies, waits for them, and re-layouts  3.74 us (1%)
    pallas_call x1, Pallas kernels, store(): pl.pallas_call(store_kernel, out_shape=tuple((jax.ShapeDtypeStruct(x.shap...  170 us
    pallas_call x1, Pallas kernels, fused(): pl.pallas_call(fused_kernel, out_shape=(pltpu.VMEM((rows, columns), f32),...  122 us

profile of v2, /device:TPU:0, one launch (start us, length us, event | category | flops | bytes accessed | tf_op | source)
XLA Modules:
  0.0 297.0 jit_solution(15170606340027804876)
XLA Ops:
  1.3 122.1 %shard_map.94 = (f32[1280,512]{1,0:T(8,128)S(1)}, f32[1280,512]{1,0:T(8,128)S(1)}, f32[160,512]{1,0:T(8,128)S(1)}) custom-call(s32[1]{0:T(128)S(6)} %copy.10.step_ref, s32[8]{0:T(128)} %plan_ref.1, f32[1280,512]{1,0:T(8,128)} %bitcast.5, f32[1280,512]{1,0:T(8,128)} %base_hbm.1, f32[160,512]{1,0:T(8,128)} %moment_hbm.1, bf16[2,384,5120]{2,1,0:T(8,128)(2,1)} %bitcast.4, ...), custom_call_target="tpu_custom_call" | custom-call | flops 8053063680 | bytes 20971520 | tf_op jit(solution)/shard_map/pallas_call | solution.py:428
  123.4 0.0 copy-start
  123.4 1.5 copy-done
  124.9 0.0 copy-start.1
  124.9 1.5 copy-done.1
  126.4 0.0 copy-start.2
  126.4 0.7 copy-done.2
  127.2 169.9 %shard_map.95 = (f32[1280,512]{1,0:T(8,128)}, f32[1280,512]{1,0:T(8,128)}, f32[160,512]{1,0:T(8,128)}) custom-call(f32[1280,512]{1,0:T(8,128)} %copy-done, f32[1280,512]{1,0:T(8,128)} %copy-done.1, f32[160,512]{1,0:T(8,128)} %copy-done.2), custom_call_target="tpu_custom_call" | custom-call | tf_op jit(solution)/shard_map/pallas_call | solution.py:407
Async XLA Ops:
  123.4 1.5 copy-start
  124.9 1.5 copy-start.1
  126.4 0.7 copy-start.2

commit v3 on v2

--- a/solution.py
+++ b/solution.py
@@ -10,6 +10,7 @@
 SCHED_LEN = 8
 INNER = 2
 MESH = pl.DeviceIdType.MESH
+PIECES = 4
 
 
 eps_norm = 1e-06
@@ -100,7 +101,8 @@
     normed, turned, full, cot, total, slopes,
     part_out, part_in, part_far, part_own, sum_out, sum_in,
     shares, shares_in, frag_rows,
-    load_sem, gather_send, gather_recv, part_send, part_recv,
+    load_sem, gather_send, gather_recv, across_send, across_recv, pass_send, pass_recv,
+    part_send, part_recv, sum_send, sum_recv,
     share_send, share_recv, frag_send, frag_recv,
 ):
     inner, shards, tokens, depth = normed.shape
@@ -159,30 +161,27 @@
         return copy
 
     def slot(k, h, i):
-        return (k * halves + h) * 3 + i
+        return (k * halves + h) * 2 + i
 
     gathers, partials, sums = {}, {}, {}
-    first_rows = depth * 3 // 4 // 16 * 16
-    pieces = (pl.ds(0, first_rows), pl.ds(first_rows, depth - first_rows))
-    last_slot = inner * halves * 3
-
-    def cast_block(k, h):
-        full[k, me, h] = weights[:, h * width : (h + 1) * width].astype(jnp.bfloat16)
-
-    def gather_across(k, h, split=False):
-        mine = full.at[k, me, h]
-        if split:
-            parts = [(mine.at[rows, :], at) for rows, at in zip(pieces, (slot(k, h, 0), last_slot))]
-        else:
-            parts = [(mine, slot(k, h, 0))]
-        gathers[k, h, 0] = [
-            send(part, part, gather_send.at[at], gather_recv.at[at], {"fsdp": across}) for part, at in parts
-        ]
+    piece_rows = depth // PIECES
+    pieces = [slice(i * piece_rows, (i + 1) * piece_rows) for i in range(PIECES)]
+
+    def piece_slot(k, h, i):
+        return (k * halves + h) * PIECES + i
+
+    def cast_rows(k, h, rows):
+        full[k, me, h, rows, :] = weights[rows, h * width : (h + 1) * width].astype(jnp.bfloat16)
+
+    def gather_across(k, h, i):
+        mine = full.at[k, me, h, pl.ds(i * piece_rows, piece_rows), :]
+        at = piece_slot(k, h, i)
+        gathers[k, h, "across", i] = send(mine, mine, across_send.at[at], across_recv.at[at], {"fsdp": across})
 
     def gather_beside(k, h):
         mine = full.at[k, me, h]
-        at = slot(k, h, 1)
-        gathers[k, h, 1] = send(mine, mine, gather_send.at[at], gather_recv.at[at], {"fsdp": partner})
+        at = k * halves + h
+        gathers[k, h, "beside"] = send(mine, mine, gather_send.at[at], gather_recv.at[at], {"fsdp": partner})
 
     def normalize_rows(k):
         rows = 16
@@ -213,16 +212,18 @@
         def term(owner):
             return jnp.dot(normed[k, owner], full[k, owner, h], preferred_element_type=jnp.float32)
 
-        for copy in gathers[k, h, 0]:
-            copy.wait_recv()
-        theirs = full.at[k, across, h]
-        at = slot(k, h, 2)
-        passed = send(theirs, theirs, gather_send.at[at], gather_recv.at[at], {"fsdp": partner})
+        passed = []
+        for i in range(PIECES):
+            gathers[k, h, "across", i].wait_recv()
+            theirs = full.at[k, across, h, pl.ds(i * piece_rows, piece_rows), :]
+            at = piece_slot(k, h, i)
+            passed.append(send(theirs, theirs, pass_send.at[at], pass_recv.at[at], {"fsdp": partner}))
         total[...] = term(me)
-        gathers[k, h, 1].wait_recv()
+        gathers[k, h, "beside"].wait_recv()
         total[...] += term(partner)
         total[...] += term(across)
-        passed.wait_recv()
+        for copy in passed:
+            copy.wait_recv()
         values = (total[...] + term(diagonal)) * inv_width
         cot_rows = cot[k, :, h * width : (h + 1) * width].astype(jnp.float32)
         slopes[...] = (cot_rows * silu_slope(values)).astype(jnp.bfloat16)
@@ -248,13 +249,16 @@
         partials[k, h] = sent
         product(across, part_far)
         sent[0].wait_recv()
-        sum_out[k, h] = (part_far[...].astype(jnp.float32) + part_in[k, h, 0].astype(jnp.float32)).astype(
-            jnp.bfloat16
-        )
-        sums[k, h] = send(
-            sum_out.at[k, h], sum_in.at[k, h],
-            part_send.at[slot(k, h, 2)], part_recv.at[slot(k, h, 2)], {"fsdp": across},
-        )
+        for i, rows in enumerate(pieces):
+            sum_out[k, h, rows, :] = (
+                part_far[rows, :].astype(jnp.float32) + part_in[k, h, 0, rows, :].astype(jnp.float32)
+            ).astype(jnp.bfloat16)
+            piece = pl.ds(i * piece_rows, piece_rows)
+            at = piece_slot(k, h, i)
+            sums[k, h, i] = send(
+                sum_out.at[k, h, piece, :], sum_in.at[k, h, piece, :],
+                sum_send.at[at], sum_recv.at[at], {"fsdp": across},
+            )
         product(me, part_own.at[h])
 
     def gradient_finish(k, h):
@@ -262,11 +266,14 @@
         cols = slice(h * width, (h + 1) * width)
         near = part_own[h].astype(jnp.float32) + part_in[k, h, 1].astype(jnp.float32)
         weights[:, cols] = weights[:, cols] - rate * near
-        sums[k, h].wait_recv()
-        if k + 1 < inner:
-            weights[:, cols] = weights[:, cols] - rate * sum_in[k, h].astype(jnp.float32)
-        else:
-            blend(h)
+        for i, rows in enumerate(pieces):
+            sums[k, h, i].wait_recv()
+            if k + 1 < inner:
+                weights[rows, cols] = weights[rows, cols] - rate * sum_in[k, h, rows, :].astype(jnp.float32)
+                cast_rows(k + 1, h, rows)
+                gather_across(k + 1, h, i)
+            else:
+                blend(h, i)
 
     fragment = plan_ref[lax.rem(step_ref[0], SCHED_LEN)]
     fragments = base.shape[1] // HEAD_DIM
@@ -337,8 +344,10 @@
                 cols = slice(j * HEAD_DIM, (j + 1) * HEAD_DIM)
                 base[at, cols] = jnp.where(chosen(share_rows, j), frag_rows[r], base[at, cols])
 
-    def blend(h):
-        @pl.loop(0, replicas)
+    def blend(h, i):
+        held = piece_rows // share_rows
+
+        @pl.loop(i * held, (i + 1) * held)
         def _(r):
             at = share_at(r)
             for j in range(h * width // HEAD_DIM, (h + 1) * width // HEAD_DIM):
@@ -349,22 +358,25 @@
                 weights[at, cols] = jnp.where(chosen(share_rows, j), mixed, trained)
 
     load_w[0].wait()
-    cast_block(0, 0)
+    cast_rows(0, 0, slice(0, depth))
     pl.semaphore_wait(barrier, replicas + 1)
-    gather_across(0, 0, split=True)
+    for i in range(PIECES):
+        gather_across(0, 0, i)
     gather_beside(0, 0)
     for h in range(1, halves):
         load_w[h].wait()
-        cast_block(0, h)
+        cast_rows(0, h, slice(0, depth))
         gather_beside(0, h)
     for copy in load_x[0]:
         copy.wait()
     normalize_rows(0)
-    ahead = gathers[0, 0, 0][0]
-    ahead.wait_send()
-    started.remove(ahead)
+    for i in range(PIECES // 2):
+        ahead = gathers[0, 0, "across", i]
+        ahead.wait_send()
+        started.remove(ahead)
     for h in range(1, halves):
-        gather_across(0, h)
+        for i in range(PIECES):
+            gather_across(0, h, i)
     load_base.wait()
     share_sent = share_start()
     turn(0)
@@ -384,8 +396,6 @@
         for h in range(halves):
             gradient_finish(k, h)
             if k + 1 < inner:
-                cast_block(k + 1, h)
-                gather_across(k + 1, h)
                 gather_beside(k + 1, h)
         if k == 0:
             fragment_finish(frag_sent)
@@ -394,22 +404,30 @@
 
 
 def store_kernel(weights, base, moment, new_weights, new_base, new_moment, store_sem):
-    pairs = ((weights, new_weights), (base, new_base), (moment, new_moment))
-    copies = [pltpu.make_async_copy(src, dst, store_sem.at[i]) for i, (src, dst) in enumerate(pairs)]
-    for copy in copies:
+    copies = []
+
+    def start(src, dst):
+        copy = pltpu.make_async_copy(src, dst, store_sem.at[len(copies)])
         copy.start()
+        copies.append(copy)
+
+    rows = weights.shape[0] // PIECES
+    for i in range(PIECES):
+        at = pl.ds(i * rows, rows)
+        start(weights.at[at, :], new_weights.at[at, :])
+        start(base.at[at, :], new_base.at[at, :])
+    start(moment, new_moment)
     for copy in copies:
         copy.wait()
 
 
 def store(*results):
-    hbm = pl.BlockSpec(memory_space=pltpu.HBM)
     return pl.pallas_call(
         store_kernel,
         out_shape=tuple(jax.ShapeDtypeStruct(x.shape, x.dtype) for x in results),
-        in_specs=[pl.BlockSpec(memory_space=pl.ANY)] * 3,
-        out_specs=(hbm,) * 3,
-        scratch_shapes=[pltpu.SemaphoreType.DMA((3,))],
+        in_specs=[pl.BlockSpec(memory_space=pltpu.VMEM)] * 3,
+        out_specs=(pl.BlockSpec(memory_space=pltpu.HBM),) * 3,
+        scratch_shapes=[pltpu.SemaphoreType.DMA((2 * PIECES + 1,))],
     )(*results)
 
 
@@ -451,10 +469,16 @@
             pltpu.VMEM((replicas - 1, share_rows, HEAD_DIM), f32),
             pltpu.VMEM((replicas, share_rows, HEAD_DIM), f32),
             dma((halves + inner * shards + 3,)),
-            dma((inner * halves * 3 + 1,)),
-            dma((inner * halves * 3 + 1,)),
-            dma((inner * halves * 3,)),
-            dma((inner * halves * 3,)),
+            dma((inner * halves,)),
+            dma((inner * halves,)),
+            dma((inner * halves * PIECES,)),
+            dma((inner * halves * PIECES,)),
+            dma((inner * halves * PIECES,)),
+            dma((inner * halves * PIECES,)),
+            dma((inner * halves * 2,)),
+            dma((inner * halves * 2,)),
+            dma((inner * halves * PIECES,)),
+            dma((inner * halves * PIECES,)),
             dma((replicas - 1,)),
             dma((replicas - 1,)),
             dma((replicas - 1,)),
@@ -476,7 +500,7 @@
 
 def fits(mesh):
     shards, replicas = mesh.shape["fsdp"], mesh.shape["replica"]
-    return shards == 4 and (D // (shards * replicas)) % 8 == 0
+    return shards == 4 and replicas % PIECES == 0 and (D // (shards * replicas)) % 8 == 0
 
 
 def solution(mesh):

time: 297 us -> 133 us (0.45)
  Pallas kernels: 292 us -> 128 us
    pallas_call x1, Pallas kernels: 170 us -> 5.04 us  [store(): pl.pallas_call(store_kernel, out_shape=tuple((jax.ShapeDtypeStruct(x.shap...]
where the time goes in v3:
time: 133 us
  Pallas kernels  128 us (96%)
  local copies, waits for them, and re-layouts  3.74 us (3%)
    pallas_call x1, Pallas kernels, fused(): pl.pallas_call(fused_kernel, out_shape=(pltpu.VMEM((rows, columns), f32),...  123 us
    pallas_call x1, Pallas kernels, store(): pl.pallas_call(store_kernel, out_shape=tuple((jax.ShapeDtypeStruct(x.shap...  5.04 us
    unnamed x6, local copies, waits for them, and re-layouts  3.74 us

profile of v3, /device:TPU:0, one launch (start us, length us, event | category | flops | bytes accessed | tf_op | source)
XLA Modules:
  0.0 132.7 jit_solution(4174464741753821671)
XLA Ops:
  1.3 122.6 %shard_map.94 = (f32[1280,512]{1,0:T(8,128)S(1)}, f32[1280,512]{1,0:T(8,128)S(1)}, f32[160,512]{1,0:T(8,128)S(1)}) custom-call(s32[1]{0:T(128)S(6)} %copy.10.step_ref, s32[8]{0:T(128)} %plan_ref.1, f32[1280,512]{1,0:T(8,128)} %bitcast.5, f32[1280,512]{1,0:T(8,128)} %base_hbm.1, f32[160,512]{1,0:T(8,128)} %moment_hbm.1, bf16[2,384,5120]{2,1,0:T(8,128)(2,1)} %bitcast.4, ...), custom_call_target="tpu_custom_call" | custom-call | flops 8053063680 | bytes 20971520 | tf_op jit(solution)/shard_map/pallas_call | solution.py:446
  123.9 0.0 copy-start
  123.9 1.5 %copy-done = f32[1280,512]{1,0:T(8,128)} copy-done((f32[1280,512]{1,0:T(8,128)}, f32[1280,512]{1,0:T(8,128)S(1)}, u32[]{:S(2)}) %copy-start) | copy-done | bytes 2621464
  125.4 0.0 copy-start.1
  125.4 1.5 %copy-done.1 = f32[1280,512]{1,0:T(8,128)} copy-done((f32[1280,512]{1,0:T(8,128)}, f32[1280,512]{1,0:T(8,128)S(1)}, u32[]{:S(2)}) %copy-start.1) | copy-done | bytes 2621464
  126.9 0.0 copy-start.2
  126.9 0.7 copy-done.2
  127.6 5.0 %shard_map.95 = (f32[1280,512]{1,0:T(8,128)}, f32[1280,512]{1,0:T(8,128)}, f32[160,512]{1,0:T(8,128)}) custom-call(f32[1280,512]{1,0:T(8,128)} %copy-done, f32[1280,512]{1,0:T(8,128)} %copy-done.1, f32[160,512]{1,0:T(8,128)} %copy-done.2), custom_call_target="tpu_custom_call" | custom-call | tf_op jit(solution)/shard_map/pallas_call | solution.py:425
Async XLA Ops:
  123.9 1.5 %copy-start = (f32[1280,512]{1,0:T(8,128)}, f32[1280,512]{1,0:T(8,128)S(1)}, u32[]{:S(2)}) copy-start(f32[1280,512]{1,0:T(8,128)S(1)} %get-tuple-element.9.weights) | copy-start | bytes 7864324
  125.4 1.5 %copy-start.1 = (f32[1280,512]{1,0:T(8,128)}, f32[1280,512]{1,0:T(8,128)S(1)}, u32[]{:S(2)}) copy-start(f32[1280,512]{1,0:T(8,128)S(1)} %get-tuple-element.10.base) | copy-start | bytes 7864324
  126.9 0.7 copy-start.2

commit v4 on v3

--- a/solution.py
+++ b/solution.py
@@ -96,9 +96,9 @@
 
 
 def fused_kernel(
-    step_ref, plan_ref, weights_hbm, base_hbm, moment_hbm, batch_hbm, cot_hbm,
+    step_hbm, plan_hbm, weights_hbm, base_hbm, moment_hbm, batch_hbm, cot_hbm,
     weights, base, moment,
-    normed, turned, full, cot, total, slopes,
+    step_ref, plan_ref, normed, turned, full, cot, total, slopes,
     part_out, part_in, part_far, part_own, sum_out, sum_in,
     shares, shares_in, frag_rows,
     load_sem, gather_send, gather_recv, across_send, across_recv, pass_send, pass_recv,
@@ -131,16 +131,22 @@
         loads.append(copy)
         return copy
 
-    def load_half(h):
-        return load(weights_hbm.at[:, block_cols(h)], weights.at[:, block_cols(h)])
-
-    load_w = [load_half(0)]
+    piece_rows = depth // PIECES
+    load_first = [
+        load(
+            weights_hbm.at[pl.ds(i * piece_rows, piece_rows), block_cols(0)],
+            weights.at[pl.ds(i * piece_rows, piece_rows), block_cols(0)],
+        )
+        for i in range(PIECES)
+    ]
     barrier = pltpu.get_barrier_semaphore()
     for other in (partner, across):
         pl.semaphore_signal(barrier, inc=1, device_id={"fsdp": other}, device_id_type=MESH)
     for offset in range(1, replicas):
         pl.semaphore_signal(barrier, inc=1, device_id={"replica": peer(offset)}, device_id_type=MESH)
-    load_w += [load_half(h) for h in range(1, halves)]
+    load_rest = [
+        load(weights_hbm.at[:, block_cols(h)], weights.at[:, block_cols(h)]) for h in range(1, halves)
+    ]
     load_x = [
         [load(batch_hbm.at[k, :, pl.ds(o * depth, depth)], normed.at[k, o]) for o in range(shards)]
         for k in range(inner)
@@ -148,6 +154,7 @@
     load_base = load(base_hbm, base)
     load_moment = load(moment_hbm, moment)
     load_cot = load(cot_hbm, cot)
+    load_small = [load(step_hbm, step_ref), load(plan_hbm, plan_ref)]
 
     started = []
 
@@ -164,7 +171,6 @@
         return (k * halves + h) * 2 + i
 
     gathers, partials, sums = {}, {}, {}
-    piece_rows = depth // PIECES
     pieces = [slice(i * piece_rows, (i + 1) * piece_rows) for i in range(PIECES)]
 
     def piece_slot(k, h, i):
@@ -275,10 +281,10 @@
             else:
                 blend(h, i)
 
-    fragment = plan_ref[lax.rem(step_ref[0], SCHED_LEN)]
     fragments = base.shape[1] // HEAD_DIM
 
     def chosen(rows, index):
+        fragment = plan_ref[lax.rem(step_ref[0], SCHED_LEN)]
         return jnp.full((rows, HEAD_DIM), fragment, jnp.int32) == index
 
     def pick(ref, at, rows):
@@ -357,14 +363,14 @@
                 mixed = mix_local * trained + (1.0 - mix_local) * frag_rows[r]
                 weights[at, cols] = jnp.where(chosen(share_rows, j), mixed, trained)
 
-    load_w[0].wait()
-    cast_rows(0, 0, slice(0, depth))
     pl.semaphore_wait(barrier, replicas + 1)
-    for i in range(PIECES):
+    for i, rows in enumerate(pieces):
+        load_first[i].wait()
+        cast_rows(0, 0, rows)
         gather_across(0, 0, i)
     gather_beside(0, 0)
     for h in range(1, halves):
-        load_w[h].wait()
+        load_rest[h - 1].wait()
         cast_rows(0, h, slice(0, depth))
         gather_beside(0, h)
     for copy in load_x[0]:
@@ -377,58 +383,36 @@
     for h in range(1, halves):
         for i in range(PIECES):
             gather_across(0, h, i)
-    load_base.wait()
-    share_sent = share_start()
     turn(0)
     load_cot.wait()
     for k in range(inner):
         for h in range(halves):
             forward(k, h)
             gradient_start(k, h)
-            if k == 0 and h == 0:
+            if h > 0:
+                continue
+            if k == 0:
                 for copy in load_x[1]:
                     copy.wait()
                 normalize_rows(1)
+            else:
+                fragment_finish(frag_sent)
         if k == 0:
-            turn(k + 1)
-            load_moment.wait()
-            frag_sent = fragment_start(share_sent)
+            for copy in load_small:
+                copy.wait()
+            load_base.wait()
+            share_sent = share_start()
         for h in range(halves):
             gradient_finish(k, h)
             if k + 1 < inner:
                 gather_beside(k + 1, h)
+            if k == 0 and h == 0:
+                turn(1)
         if k == 0:
-            fragment_finish(frag_sent)
+            load_moment.wait()
+            frag_sent = fragment_start(share_sent)
     for copy in started:
         copy.wait_send()
-
-
-def store_kernel(weights, base, moment, new_weights, new_base, new_moment, store_sem):
-    copies = []
-
-    def start(src, dst):
-        copy = pltpu.make_async_copy(src, dst, store_sem.at[len(copies)])
-        copy.start()
-        copies.append(copy)
-
-    rows = weights.shape[0] // PIECES
-    for i in range(PIECES):
-        at = pl.ds(i * rows, rows)
-        start(weights.at[at, :], new_weights.at[at, :])
-        start(base.at[at, :], new_base.at[at, :])
-    start(moment, new_moment)
-    for copy in copies:
-        copy.wait()
-
-
-def store(*results):
-    return pl.pallas_call(
-        store_kernel,
-        out_shape=tuple(jax.ShapeDtypeStruct(x.shape, x.dtype) for x in results),
-        in_specs=[pl.BlockSpec(memory_space=pltpu.VMEM)] * 3,
-        out_specs=(pl.BlockSpec(memory_space=pltpu.HBM),) * 3,
-        scratch_shapes=[pltpu.SemaphoreType.DMA((2 * PIECES + 1,))],
-    )(*results)
 
 
 def fused(local_weights, outer_base, outer_momentum, batch, cotangent, step, plan):
@@ -440,7 +424,6 @@
     width = columns // halves
     f32, bf16 = jnp.float32, jnp.bfloat16
     hbm = pl.BlockSpec(memory_space=pltpu.HBM)
-    smem = pl.BlockSpec(memory_space=pltpu.SMEM)
     dma = pltpu.SemaphoreType.DMA
     flops = inner * 4 * tokens * features * columns
     return pl.pallas_call(
@@ -450,9 +433,11 @@
             pltpu.VMEM((rows, columns), f32),
             pltpu.VMEM((share_rows, columns), f32),
         ),
-        in_specs=[smem, smem] + [hbm] * 5,
+        in_specs=[hbm] * 7,
         out_specs=(pl.BlockSpec(memory_space=pltpu.VMEM),) * 3,
         scratch_shapes=[
+            pltpu.SMEM(step.shape, jnp.int32),
+            pltpu.SMEM(plan.shape, jnp.int32),
             pltpu.VMEM((inner, shards, tokens, rows), bf16),
             pltpu.VMEM((shards, rows, tokens), bf16),
             pltpu.VMEM((inner, shards, halves, rows, width), bf16),
@@ -468,7 +453,7 @@
             pltpu.VMEM((replicas, share_rows, HEAD_DIM), f32),
             pltpu.VMEM((replicas - 1, share_rows, HEAD_DIM), f32),
             pltpu.VMEM((replicas, share_rows, HEAD_DIM), f32),
-            dma((halves + inner * shards + 3,)),
+            dma((PIECES + halves - 1 + inner * shards + 5,)),
             dma((inner * halves,)),
             dma((inner * halves,)),
             dma((inner * halves * PIECES,)),
@@ -494,7 +479,7 @@
 
 
 def on_device_fused(*args):
-    new_weights, new_base, new_momentum = store(*fused(*args))
+    new_weights, new_base, new_momentum = fused(*args)
     return (new_weights[None], new_base, new_momentum)
 
 

time: 133 us -> 127 us (0.955)
  Pallas kernels: 128 us -> 122 us
    pallas_call x1 -> x0, Pallas kernels: 5.04 us -> none  [store(): pl.pallas_call(store_kernel, out_shape=tuple((jax.ShapeDtypeStruct(x.shap...]
    unnamed x6 -> x3, local copies, waits for them, and re-layouts: 3.74 us -> 3.71 us
where the time goes in v4:
time: 127 us
  Pallas kernels  122 us (96%)
  local copies, waits for them, and re-layouts  3.71 us (3%)
  between operations  1.29 us (1%)
    pallas_call x1, Pallas kernels, fused(): pl.pallas_call(fused_kernel, out_shape=(pltpu.VMEM((rows, columns), f32),...  122 us
    unnamed x3, local copies, waits for them, and re-layouts  3.71 us

profile of v4, /device:TPU:0, one launch (start us, length us, event | category | flops | bytes accessed | tf_op | source)
XLA Modules:
  0.0 127.0 jit_solution(8671163091695917827)
XLA Ops:
  1.3 122.0 %shard_map.94 = (f32[1280,512]{1,0:T(8,128)S(1)}, f32[1280,512]{1,0:T(8,128)S(1)}, f32[160,512]{1,0:T(8,128)S(1)}) custom-call(s32[1]{0:T(128)S(6)} %copy.16.step_hbm, s32[8]{0:T(128)} %plan_hbm.1, f32[1280,512]{1,0:T(8,128)} %bitcast.6, f32[1280,512]{1,0:T(8,128)} %base_hbm.1, f32[160,512]{1,0:T(8,128)} %moment_hbm.1, bf16[2,384,5120]{2,1,0:T(8,128)(2,1)} %bitcast.5, ...), custom_call_target="tpu_custom_call" | custom-call | flops 8053063680 | bytes 20971520 | tf_op jit(solution)/shard_map/pallas_call | solution.py:429
  123.3 1.5 %copy.13 = f32[1,1280,512]{2,1,0:T(8,128)} copy(f32[1,1280,512]{2,1,0:T(8,128)S(1)} %bitcast.4) | data formatting | bytes 5242880
  124.8 0.7 copy.15
  125.5 1.5 %copy.14 = f32[1280,512]{1,0:T(8,128)} copy(f32[1280,512]{1,0:T(8,128)S(1)} %get-tuple-element.10) | data formatting | bytes 5242880

commit v5 on v4

--- a/solution.py
+++ b/solution.py
@@ -243,16 +243,14 @@
             ).astype(jnp.bfloat16)
 
     def gradient_start(k, h):
-        sent = []
-        for i, owner in enumerate((diagonal, partner)):
+        def hand_over(i, owner):
             product(owner, part_out.at[k, h, i])
-            sent.append(
-                send(
-                    part_out.at[k, h, i], part_in.at[k, h, i],
-                    part_send.at[slot(k, h, i)], part_recv.at[slot(k, h, i)], {"fsdp": partner},
-                )
+            return send(
+                part_out.at[k, h, i], part_in.at[k, h, i],
+                part_send.at[slot(k, h, i)], part_recv.at[slot(k, h, i)], {"fsdp": partner},
             )
-        partials[k, h] = sent
+
+        sent = [hand_over(0, diagonal)]
         product(across, part_far)
         sent[0].wait_recv()
         for i, rows in enumerate(pieces):
@@ -265,6 +263,8 @@
                 sum_out.at[k, h, piece, :], sum_in.at[k, h, piece, :],
                 sum_send.at[at], sum_recv.at[at], {"fsdp": across},
             )
+        sent.append(hand_over(1, partner))
+        partials[k, h] = sent
         product(me, part_own.at[h])
 
     def gradient_finish(k, h):

time: 127 us -> 127 us (level)
  no operation moved by 1% of the time
where the time goes in v5:
time: 127 us
  Pallas kernels  122 us (96%)
  local copies, waits for them, and re-layouts  3.71 us (3%)
  between operations  1.29 us (1%)
    pallas_call x1, Pallas kernels, fused(): pl.pallas_call(fused_kernel, out_shape=(pltpu.VMEM((rows, columns), f32),...  122 us
    unnamed x3, local copies, waits for them, and re-layouts  3.71 us

profile of v5, /device:TPU:0, one launch (start us, length us, event | category | flops | bytes accessed | tf_op | source)
XLA Modules:
  0.0 127.0 jit_solution(7566621433321581166)
XLA Ops:
  1.3 122.0 %shard_map.94 = (f32[1280,512]{1,0:T(8,128)S(1)}, f32[1280,512]{1,0:T(8,128)S(1)}, f32[160,512]{1,0:T(8,128)S(1)}) custom-call(s32[1]{0:T(128)S(6)} %copy.16.step_hbm, s32[8]{0:T(128)} %plan_hbm.1, f32[1280,512]{1,0:T(8,128)} %bitcast.6, f32[1280,512]{1,0:T(8,128)} %base_hbm.1, f32[160,512]{1,0:T(8,128)} %moment_hbm.1, bf16[2,384,5120]{2,1,0:T(8,128)(2,1)} %bitcast.5, ...), custom_call_target="tpu_custom_call" | custom-call | flops 8053063680 | bytes 20971520 | tf_op jit(solution)/shard_map/pallas_call | solution.py:429
  123.3 1.5 %copy.13 = f32[1,1280,512]{2,1,0:T(8,128)} copy(f32[1,1280,512]{2,1,0:T(8,128)S(1)} %bitcast.4) | data formatting | bytes 5242880
  124.8 0.7 copy.15
  125.5 1.5 %copy.14 = f32[1280,512]{1,0:T(8,128)} copy(f32[1280,512]{1,0:T(8,128)S(1)} %get-tuple-element.10) | data formatting | bytes 5242880
